TPU v7x, 512 devices: a whole 4x4x16 slice. The times are simulated.
512 devices in a mesh: ctx: 16 (over z_lo, x), fsdp: 32 (over y, z_hi, core).
Axes of the slice: x: 4, y: 4, z: 16 (z_hi: 4, z_lo: 4; z = z_hi * 4 + z_lo), core: 2. Of those that a mesh axis runs over, the one named last changes fastest.
Arguments:
- queries: bfloat16 [6144, 4096], P('ctx', 'fsdp'), may hold values from -8 to 8
- keys: bfloat16 [6144, 4096], P('ctx', 'fsdp'), may hold values from -8 to 8
- values: bfloat16 [6144, 4096], P('ctx', 'fsdp'), may hold values from -6 to 6
- query_tangent: bfloat16 [6144, 4096], P('ctx', 'fsdp'), may hold values from -6 to 6
- key_tangent: bfloat16 [6144, 4096], P('ctx', 'fsdp'), may hold values from -6 to 6
- value_tangent: bfloat16 [6144, 4096], P('ctx', 'fsdp'), may hold values from -6 to 6
- out_weight: bfloat16 [4096, 5120], P('fsdp'), may hold values from -0.09375 to 0.09375
Outputs:
- projected: bfloat16 [6144, 5120], P('ctx', 'fsdp')
- projected_tangent: bfloat16 [6144, 5120], P('ctx', 'fsdp')
All inputs are finite; a program needn't handle non-finite values.
Results may differ from a plain program's by a relative error of at most 0.024.
Values may be sent and summed in bfloat16 or wider, within the bound.
A program may use at most 128 MiB of HBM per device.

v0:
```python
import jax
import jax.numpy as jnp
from jax import lax
from jax.sharding import PartitionSpec as P

HD = 128


def fetch_columns(out_weight):
    return lax.all_to_all(out_weight, "fsdp", split_axis=1, concat_axis=0, tiled=True)


def body(queries, keys, values, query_tangent, key_tangent, value_tangent, out_weight):
    local_tokens = queries.shape[0]
    feat_local = queries.shape[1]
    heads = feat_local // HD
    scale = 1.0 / HD**0.5
    query_heads = queries.reshape(local_tokens, heads, HD)
    query_steps = query_tangent.reshape(local_tokens, heads, HD)
    start_top = jnp.full((heads, local_tokens), -1e30, jnp.float32)
    pieces = (
        lax.all_gather(keys, "ctx", axis=0, tiled=True),
        lax.all_gather(values, "ctx", axis=0, tiled=True),
        lax.all_gather(key_tangent, "ctx", axis=0, tiled=True),
        lax.all_gather(value_tangent, "ctx", axis=0, tiled=True),
    )
    running_top = start_top
    count = pieces[0].shape[0]
    key_part, value_part, key_step, value_step = [p.reshape(count, heads, HD) for p in pieces]
    scores = (
        jnp.einsum("thd,nhd->htn", query_heads, key_part, preferred_element_type=jnp.float32)
        * scale
    )
    score_tangent = (
        jnp.einsum("thd,nhd->htn", query_steps, key_part, preferred_element_type=jnp.float32)
        + jnp.einsum("thd,nhd->htn", query_heads, key_step, preferred_element_type=jnp.float32)
    ) * scale
    new_top = jnp.maximum(running_top, jnp.max(scores, axis=-1))
    weights = jnp.exp(scores - new_top[..., None])
    spread = weights * score_tangent
    weights_reduced = weights.astype(jnp.bfloat16)
    spread_reduced = spread.astype(jnp.bfloat16)
    primal_acc = jnp.einsum(
        "htn,nhd->htd", weights_reduced, value_part, preferred_element_type=jnp.float32
    )
    tangent_acc = jnp.einsum(
        "htn,nhd->htd", weights_reduced, value_step, preferred_element_type=jnp.float32
    ) + jnp.einsum("htn,nhd->htd", spread_reduced, value_part, preferred_element_type=jnp.float32)
    running_total = jnp.sum(weights, axis=-1)
    running_spread = jnp.sum(spread, axis=-1)
    folded = (new_top, running_total, running_spread, primal_acc, tangent_acc)
    running_top, running_total, running_spread, primal_acc, tangent_acc = folded
    mixed = primal_acc / running_total[..., None]
    mixed_tangent = (
        tangent_acc / running_total[..., None] - (running_spread / running_total)[..., None] * mixed
    )
    mixed = jnp.transpose(mixed, (1, 0, 2)).reshape(local_tokens, feat_local).astype(jnp.bfloat16)
    mixed_tangent = (
        jnp.transpose(mixed_tangent, (1, 0, 2))
        .reshape(local_tokens, feat_local)
        .astype(jnp.bfloat16)
    )
    weight_cols = fetch_columns(out_weight)
    mixed_all, tangent_all = (
        lax.all_gather(mixed, "fsdp", axis=1, tiled=True),
        lax.all_gather(mixed_tangent, "fsdp", axis=1, tiled=True),
    )
    projected = jnp.dot(mixed_all, weight_cols, preferred_element_type=jnp.float32)
    projected_tangent = jnp.dot(tangent_all, weight_cols, preferred_element_type=jnp.float32)
    return (projected.astype(jnp.bfloat16), projected_tangent.astype(jnp.bfloat16))


def solution(mesh):
    in_specs = (
        P("ctx", "fsdp"),
        P("ctx", "fsdp"),
        P("ctx", "fsdp"),
        P("ctx", "fsdp"),
        P("ctx", "fsdp"),
        P("ctx", "fsdp"),
        P("fsdp", None),
    )
    out_specs = (P("ctx", "fsdp"), P("ctx", "fsdp"))
    return jax.shard_map(body, mesh=mesh, in_specs=in_specs, out_specs=out_specs, check_vma=False)
```

profile of v0, /device:TPU:1, one launch (start us, length us, event | category | flops | bytes accessed | tf_op | source)
XLA Modules:
  0.0 607.0 jit_solution(13879902392085382088)
XLA Ops:
  7.2 0.7 all-gather.7.cloned.1.call-update
  8.0 0.7 all-gather.9.cloned.1.call-update
  8.7 0.7 all-gather.15.cloned.1.call-update
  9.4 0.5 all-gather.13.cloned.1.call-update
  10.0 82.4 %all-gather.7.cloned.1.call-done = bf16[6144,128]{1,0:T(8,128)(2,1)} async-done(((bf16[384,128]{1,0:T(8,128)(2,1)}), bf16[6144,128]{1,0:T(8,128)(2,1)}) %all-gather.7.cloned.1.call-update) | async-done | bytes 1572880 | tf_op jit(solution)/shard_map/all_gather | solution.py:22
  92.5 2.9 fusion.28
  95.4 3.6 copy-done.1
  99.0 4.3 fusion
  103.3 76.9 %all-gather.9.cloned.1.call-done = bf16[6144,128]{1,0:T(8,128)(2,1)} async-done(((bf16[384,128]{1,0:T(8,128)(2,1)}), bf16[6144,128]{1,0:T(8,128)(2,1)}) %all-gather.9.cloned.1.call-update) | async-done | bytes 1572880 | tf_op jit(solution)/shard_map/all_gather | solution.py:23
  180.2 5.0 fusion.29
  185.2 0.0 all-gather.17.cloned.1.call-start
  185.3 5.1 fusion.32
  190.3 77.6 %all-gather.15.cloned.1.call-done = bf16[6144,128]{1,0:T(8,128)(2,1)} async-done(((bf16[384,128]{1,0:T(8,128)(2,1)}), bf16[6144,128]{1,0:T(8,128)(2,1)}) %all-gather.15.cloned.1.call-update) | async-done | bytes 1572880 | tf_op jit(solution)/shard_map/all_gather | solution.py:24
  267.9 10.8 %fusion.30 = (f32[384]{0:T(512)S(1)}, bf16[384,6144]{1,0:T(8,128)(2,1)}) fusion(f32[384,6144]{1,0:T(8,128)} %fusion.32, bf16[384,128]{1,0:T(8,128)(2,1)S(1)} %copy-done, bf16[6144,128]{1,0:T(8,128)(2,1)} %all-gather.15.cloned.1.call-done, f32[384,6144]{1,0:T(8,128)} %copy-done.1, f32[384]{0:T(512)S(1)} %broadcast_maximum_fusion), kind=kOutput, calls=%fused_computation.23 | convolution fusion | flops 618135168 | bytes 25267200 | tf_op jit(solution)/shard_map/thd,nhd->htn/dot_general | solution.py:36
  278.7 76.7 %all-gather.13.cloned.1.call-done = bf16[6144,128]{1,0:T(8,128)(2,1)} async-done(((bf16[384,128]{1,0:T(8,128)(2,1)}), bf16[6144,128]{1,0:T(8,128)(2,1)}) %all-gather.13.cloned.1.call-update) | async-done | bytes 1572880 | tf_op jit(solution)/shard_map/all_gather | solution.py:25
  355.5 4.3 fusion.31
  359.8 0.3 copy-done.6
  360.2 2.0 fusion.25
  362.2 0.8 copy.9
  363.0 91.7 %all_to_all.19 = bf16[128,32,160]{0,2,1:T(8,128)(2,1)S(1)} all-to-all(bf16[128,32,160]{0,2,1:T(8,128)(2,1)S(1)} %bitcast.32), channel_id=1, replica_groups=mesh['ctx'=16,'fsdp'=32] {'fsdp'}, dimensions={1} | all-to-all | bytes 2621440 | tf_op jit(solution)/shard_map/all_to_all | solution.py:10
  454.8 53.1 %all-gather.11.cloned.1.call-done = bf16[384,4096]{1,0:T(8,128)(2,1)} async-done(((bf16[384,128]{1,0:T(8,128)(2,1)}), bf16[384,4096]{1,0:T(8,128)(2,1)}) %all-gather.11.cloned.1.call-update) | async-done | bytes 3145744 | tf_op jit(solution)/shard_map/all_gather | solution.py:65
  507.9 3.7 fusion.13
  511.5 85.0 %all-gather.17.cloned.1.call-done = bf16[384,4096]{1,0:T(8,128)(2,1)} async-done(((bf16[384,128]{1,0:T(8,128)(2,1)}), bf16[384,4096]{1,0:T(8,128)(2,1)}) %all-gather.17.cloned.1.call-update) | async-done | bytes 3145744 | tf_op jit(solution)/shard_map/all_gather | solution.py:66
  596.5 3.7 fusion.16
  (21 shorter events, 0.3 us)
Async XLA Ops:
  7.2 85.3 %copy-start = (bf16[384,128]{1,0:T(8,128)(2,1)S(1)}, bf16[384,128]{1,0:T(8,128)(2,1)}, u32[]{:S(2)}) copy-start(bf16[384,128]{1,0:T(8,128)(2,1)} %param.7) | copy-start | bytes 294916
  7.2 85.3 %all-gather.7.cloned.1.call-start = ((), (), s32[]{:S(2)}) async-start(), calls=%async_computation.1 | async-start | bytes 1671168 | tf_op jit(solution)/shard_map/all_gather | solution.py:22
  7.9 172.3 %all-gather.9.cloned.1.call-start = ((), (), s32[]{:S(2)}) async-start(), calls=%async_computation.2 | async-start | bytes 1671168 | tf_op jit(solution)/shard_map/all_gather | solution.py:23
  8.7 259.2 %all-gather.15.cloned.1.call-start = ((), (), s32[]{:S(2)}) async-start(), calls=%async_computation.5 | async-start | bytes 1671168 | tf_op jit(solution)/shard_map/all_gather | solution.py:24
  9.4 346.1 %all-gather.13.cloned.1.call-start = ((), (), s32[]{:S(2)}) async-start(), calls=%async_computation.4 | async-start | bytes 1671168 | tf_op jit(solution)/shard_map/all_gather | solution.py:25
  10.0 497.9 %all-gather.11.cloned.1.call-start = ((), (), s32[]{:S(2)}) async-start(), calls=%async_computation.3 | async-start | bytes 3244032 | tf_op jit(solution)/shard_map/all_gather | solution.py:65
  95.3 3.7 copy-start.1
  180.2 5.1 copy-start.2
  180.2 5.1 copy-start.5
  185.2 411.4 %all-gather.17.cloned.1.call-start = ((), (), s32[]{:S(2)}) async-start(), calls=%async_computation.6 | async-start | bytes 3244032 | tf_op jit(solution)/shard_map/all_gather | solution.py:66
  355.5 4.4 copy-start.3
  355.5 4.7 copy-start.6
  360.2 2.1 copy-start.4
Sparse Core Ops, SparseCore 0:
  10.1 82.3 all-gather.6
  94.5 85.5 all-gather.8
  182.3 85.5 all-gather.14
  269.8 85.5 all-gather.12
  358.9 148.8 all-gather.10
  510.8 85.7 all-gather.16
where the time goes:
time: 607 us
  waiting for transfers between devices  454 us (75%)
  blocking collectives  91.7 us (15%)
  matrix products  37.5 us (6%)
  between operations  14.2 us (2%)
    all_to_all x1, blocking collectives, fetch_columns(): lax.all_to_all(out_weight, 'fsdp', split_axis=1, concat_axis=0, tiled=True)  91.7 us
    all_gather x1, waiting for transfers between devices, body(): lax.all_gather(mixed_tangent, 'fsdp', axis=1, tiled=True)  85 us
    all_gather x1, waiting for transfers between devices, body(): lax.all_gather(keys, 'ctx', axis=0, tiled=True)  82.4 us
    all_gather x1, waiting for transfers between devices, body(): lax.all_gather(key_tangent, 'ctx', axis=0, tiled=True)  77.6 us
    all_gather x1, waiting for transfers between devices, body(): lax.all_gather(values, 'ctx', axis=0, tiled=True)  76.9 us
    all_gather x1, waiting for transfers between devices, body(): lax.all_gather(value_tangent, 'ctx', axis=0, tiled=True)  76.7 us
    all_gather x1, waiting for transfers between devices, body(): lax.all_gather(mixed, 'fsdp', axis=1, tiled=True)  53.1 us
  transfers between devices with their start and end apart: 6, of which 6 were waited for; matrix products, arithmetic and copies ran while one was open for 6% of the time, Pallas kernels for 0%

commit v1 on v0

v1 whole, which is shorter than its diff:
```python
import functools

import jax
import jax.numpy as jnp
from jax import lax
from jax.experimental import pallas as pl
from jax.experimental.pallas import tpu as pltpu
from jax.sharding import PartitionSpec as P

MESH = pl.DeviceIdType.MESH
HD = 128
F32 = jnp.float32
BF16 = jnp.bfloat16
DIMS = (4, 4, 4, 4, 2)


def nt_dot(a, b):
    return lax.dot_general(a, b, (((1,), (1,)), ((), ())), preferred_element_type=F32)


def kernel(
    dims,
    q_ref, k_ref, v_ref, dq_ref, dk_ref, dv_ref, w_ref,
    out_ref, dout_ref,
    qd_all, kd_all, vt_own, vt_all, wt_own, wt_all,
    part, stats, part_in, stats_in, mix, x_all, send_z, recv_z, swap_out, swap_in,
    q_s, q_r, k_s, k_r, v_s, v_r, w_s, w_r, p_s, p_r, t_s, t_r, x_s, x_r, z_s, z_r, c_s, c_r, l_s,
):
    nx, nz, ny, nh, nc = dims
    tok = q_ref.shape[0]
    col = out_ref.shape[1]
    scale = 1.0 / HD**0.5
    rate = scale * 1.4426950408889634

    ctx = lax.axis_index("ctx")
    fsdp = lax.axis_index("fsdp")
    zl, x = ctx // nx, lax.rem(ctx, nx)
    core = lax.rem(fsdp, nc)
    zh = lax.rem(fsdp // nc, nh)
    y = fsdp // (nc * nh)

    def at_x(d):
        return (zl * nx + lax.rem(x + d, nx), fsdp)

    def at_zl(d):
        return (lax.rem(zl + d, nz) * nx + x, fsdp)

    def at_zh(d):
        return (ctx, (y * nh + lax.rem(zh + d, nh)) * nc + core)

    def at_yc(e):
        return (ctx, (lax.rem(y + e // nc, ny) * nh + zh) * nc + lax.rem(core + e % nc, nc))

    partners = (
        [at_x(d) for d in range(1, nx)]
        + [at_zl(d) for d in range(1, nz)]
        + [at_zh(d) for d in range(1, nh)]
        + [at_yc(e) for e in range(1, ny * nc)]
    )
    barrier = pltpu.get_barrier_semaphore()
    for device in partners:
        pl.semaphore_signal(barrier, inc=1, device_id=device, device_id_type=MESH)

    key_rows = pl.ds(pl.multiple_of(x * tok, tok), tok)
    kd_all[key_rows, 0:HD] = k_ref[...]
    kd_all[key_rows, HD : 2 * HD] = dk_ref[...]
    qd_all[zl, :, 0:HD] = dq_ref[...]
    qd_all[zl, :, HD : 2 * HD] = q_ref[...]
    vt_own[0:HD, :] = v_ref[...].T
    vt_own[HD : 2 * HD, :] = dv_ref[...].T

    pl.semaphore_wait(barrier, len(partners))

    def remote(src, dst, s, r, device):
        return pltpu.make_async_remote_copy(
            src_ref=src, dst_ref=dst, send_sem=s, recv_sem=r, device_id=device, device_id_type=MESH
        )

    q_copies = [
        remote(qd_all.at[zl], qd_all.at[zl], q_s.at[d - 1], q_r.at[d - 1], at_zl(d))
        for d in range(1, nz)
    ]
    k_copies = [
        remote(kd_all.at[key_rows], kd_all.at[key_rows], k_s.at[d - 1], k_r.at[d - 1], at_x(d))
        for d in range(1, nx)
    ]
    v_copies = [
        remote(vt_own, vt_all.at[:, key_rows], v_s.at[d - 1], v_r.at[d - 1], at_x(d))
        for d in range(1, nx)
    ]
    for copy in q_copies + k_copies + v_copies:
        copy.start()
    v_local = pltpu.make_async_copy(vt_own, vt_all.at[:, key_rows], l_s.at[0])
    v_local.start()

    group = nh * nc * col
    for i in range(ny):
        wt_own[i * group : (i + 1) * group, :] = w_ref[:, i * group : (i + 1) * group].T
    slot = y * nc + core
    slot_cols = pl.ds(pl.multiple_of(slot * HD, HD), HD)

    def weight_rows(row):
        return pl.ds(pl.multiple_of(row * group, group), group)

    w_copies = [
        remote(
            wt_own.at[weight_rows(lax.rem(y + e // nc, ny))],
            wt_all.at[:, slot_cols],
            w_s.at[e - 1],
            w_r.at[e - 1],
            at_yc(e),
        )
        for e in range(1, ny * nc)
    ]
    for copy in w_copies:
        copy.start()
    w_local = pltpu.make_async_copy(wt_own.at[weight_rows(y)], wt_all.at[:, slot_cols], l_s.at[1])
    w_local.start()

    for copy in q_copies + k_copies + v_copies:
        copy.wait()
    v_local.wait()

    def attend(j, carry):
        owner = lax.rem(zl + j + 1, nz)
        qd = qd_all[owner]
        scores = nt_dot(kd_all[:, 0:HD], qd[:, HD : 2 * HD])
        steps = nt_dot(kd_all[...], qd)
        top = jnp.max(scores, axis=0, keepdims=True)
        weights = jnp.exp2((scores - top) * rate)
        spread = weights * steps
        total = jnp.sum(weights, axis=0, keepdims=True)
        mean = jnp.sum(spread, axis=0, keepdims=True) * scale / total
        first = jnp.dot(vt_all[...], weights.astype(BF16), preferred_element_type=F32)
        second = jnp.dot(vt_all[0:HD, :], spread.astype(BF16), preferred_element_type=F32)
        mixed = first[0:HD] / total
        part[j, 0:HD, :] = mixed.astype(BF16)
        part[j, HD : 2 * HD, :] = (
            (first[HD : 2 * HD] + second * scale) / total - mean * mixed
        ).astype(BF16)
        stats[j, 0:1, :] = top * rate
        stats[j, 1:2, :] = total
        stats[j, 2:3, :] = mean
        stats[j, 3:8, :] = jnp.zeros((5, tok), F32)

        @pl.when(j < nz - 1)
        def _():
            device = (owner * nx + x, fsdp)
            remote(part.at[j], part_in.at[j], p_s.at[j], p_r.at[j], device).start()
            remote(stats.at[j], stats_in.at[j], t_s.at[j], t_r.at[j], device).start()

        return carry

    lax.fori_loop(0, nz, attend, 0)

    for j in range(nz - 1):
        remote(part.at[j], part_in.at[j], p_s.at[j], p_r.at[j], at_zl(j + 1)).wait()
        remote(stats.at[j], stats_in.at[j], t_s.at[j], t_r.at[j], at_zl(j + 1)).wait()

    parts = [(part_in.at[j], stats_in.at[j]) for j in range(nz - 1)]
    parts.append((part.at[nz - 1], stats.at[nz - 1]))
    tops = [s[0:1, :] for _, s in parts]
    top = functools.reduce(jnp.maximum, tops)
    shares = [jnp.exp2(t - top) * s[1:2, :] for t, (_, s) in zip(tops, parts)]
    total = sum(shares)
    shares = [s / total for s in shares]
    means = [s[2:3, :] for _, s in parts]
    mean = sum(a * b for a, b in zip(shares, means))
    mixed = jnp.zeros((HD, tok), F32)
    tangent = jnp.zeros((HD, tok), F32)
    for share, here, (p, _) in zip(shares, means, parts):
        one = p[0:HD, :].astype(F32)
        mixed += share * one
        tangent += share * (p[HD : 2 * HD, :].astype(F32) + (here - mean) * one)
    mix[0] = mixed.astype(BF16)
    mix[1] = tangent.astype(BF16)

    slot_rows = pl.ds(pl.multiple_of(slot * HD, HD), HD)
    x_copies = [
        remote(
            mix.at[lax.rem(core + e % nc, nc)],
            x_all.at[slot_rows],
            x_s.at[e - 1],
            x_r.at[e - 1],
            at_yc(e),
        )
        for e in range(1, ny * nc)
    ]
    for copy in x_copies:
        copy.start()
    x_all[slot_rows, :] = mix[core]
    for copy in w_copies + x_copies:
        copy.wait()
    w_local.wait()

    block = nc * col

    def project(d):
        rows = pl.ds(pl.multiple_of(lax.rem(zh + d, nh) * block, block), block)
        return jnp.dot(wt_all[rows, :], x_all[...], preferred_element_type=F32)

    z_copies = []
    for d in range(1, nh):
        send_z[d - 1] = project(d).astype(BF16)
        copy = remote(send_z.at[d - 1], recv_z.at[d - 1], z_s.at[d - 1], z_r.at[d - 1], at_zh(d))
        copy.start()
        z_copies.append(copy)
    total = project(0)
    for d in range(1, nh):
        z_copies[d - 1].wait()
        total += recv_z[d - 1].astype(F32)
    swap_out[...] = total.astype(BF16)

    other = lax.rem(core + 1, nc)

    def cols(c):
        return pl.ds(pl.multiple_of(c * col, col), col)

    copy = remote(swap_out.at[cols(other)], swap_in, c_s, c_r, at_yc(1))
    copy.start()
    mine = swap_out[cols(core), :]
    copy.wait()
    theirs = swap_in[...]
    out_ref[...] = jnp.where(core == 0, mine, theirs).T
    dout_ref[...] = jnp.where(core == 0, theirs, mine).T


def call(dims, q, k, v, dq, dk, dv, w):
    nx, nz, ny, nh, nc = dims
    tok = q.shape[0]
    col = w.shape[1] // (ny * nh * nc)
    block = nc * col
    group = nh * block
    peers = ny * nc
    dma = pltpu.SemaphoreType.DMA
    vmem = pl.BlockSpec(memory_space=pltpu.VMEM)

    def pair(n):
        return [dma((max(n, 1),)), dma((max(n, 1),))]

    return pl.pallas_call(
        functools.partial(kernel, dims),
        out_shape=(
            jax.ShapeDtypeStruct((tok, col), BF16),
            jax.ShapeDtypeStruct((tok, col), BF16),
        ),
        in_specs=[vmem] * 7,
        out_specs=(vmem, vmem),
        scratch_shapes=[
            pltpu.VMEM((nz, tok, 2 * HD), BF16),
            pltpu.VMEM((nx * tok, 2 * HD), BF16),
            pltpu.VMEM((2 * HD, tok), BF16),
            pltpu.VMEM((2 * HD, nx * tok), BF16),
            pltpu.VMEM((w.shape[1], HD), BF16),
            pltpu.VMEM((group, peers * HD), BF16),
            pltpu.VMEM((nz, 2 * HD, tok), BF16),
            pltpu.VMEM((nz, 8, tok), F32),
            pltpu.VMEM((max(nz - 1, 1), 2 * HD, tok), BF16),
            pltpu.VMEM((max(nz - 1, 1), 8, tok), F32),
            pltpu.VMEM((2, HD, tok), BF16),
            pltpu.VMEM((peers * HD, tok), BF16),
            pltpu.VMEM((max(nh - 1, 1), block, tok), BF16),
            pltpu.VMEM((max(nh - 1, 1), block, tok), BF16),
            pltpu.VMEM((block, tok), BF16),
            pltpu.VMEM((col, tok), BF16),
        ]
        + pair(nz - 1)
        + pair(nx - 1)
        + pair(nx - 1)
        + pair(peers - 1)
        + pair(nz - 1)
        + pair(nz - 1)
        + pair(peers - 1)
        + pair(nh - 1)
        + [dma, dma, dma((2,))],
        compiler_params=pltpu.CompilerParams(
            collective_id=0, has_side_effects=True, vmem_limit_bytes=56 * 1024 * 1024
        ),
        name="attend_and_project",
    )(q, k, v, dq, dk, dv, w)


def solution(mesh, dims=DIMS):
    spec = P("ctx", "fsdp")
    return jax.shard_map(
        functools.partial(call, dims),
        mesh=mesh,
        in_specs=(spec,) * 6 + (P("fsdp", None),),
        out_specs=(spec, spec),
        check_vma=False,
    )
```

time: 607 us -> 119 us (0.20)
  the two profiles are of different devices: /device:TPU:1 before, /device:TPU:33 now
where the time goes in v1:
time: 119 us
  Pallas kernels  115 us (97%)
  local copies, waits for them, and re-layouts  3.38 us (3%)
    pallas_call x1, Pallas kernels, call(): pl.pallas_call(functools.partial(kernel, dims), out_shape=(jax.ShapeDtype...  115 us
    pallas_call x2, local copies, waits for them, and re-layouts, call(): pl.pallas_call(functools.partial(kernel, dims), out_shape=(jax.ShapeDtype...  3.38 us

profile of v1, /device:TPU:33, one launch (start us, length us, event | category | flops | bytes accessed | tf_op | source)
XLA Modules:
  0.0 118.9 jit_solution(646531610257152657)
XLA Ops:
  0.6 114.9 %attend_and_project.1 = (bf16[384,160]{1,0:T(8,128)(2,1)}, bf16[384,160]{1,0:T(8,128)(2,1)}) custom-call(bf16[384,128]{1,0:T(8,128)(2,1)} %q_ref.1, bf16[384,128]{1,0:T(8,128)(2,1)} %k_ref.1, bf16[384,128]{1,0:T(8,128)(2,1)} %v_ref.1, bf16[384,128]{1,0:T(8,128)(2,1)} %dq_ref.1, bf16[384,128]{1,0:T(8,128)(2,1)} %dk_ref.1, bf16[384,128]{1,0:T(8,128)(2,1)} %dv_ref.1, ...), custom_call_target="tpu_custom_call" | custom-call | tf_op jit(solution)/shard_map/attend_and_project/pallas_call | solution.py:241
  115.5 1.7 %copy.9 = bf16[384,160]{0,1:T(8,128)(2,1)} copy(bf16[384,160]{1,0:T(8,128)(2,1)} %get-tuple-element.2) | data formatting | bytes 245760 | tf_op jit(solution)/shard_map/attend_and_project/pallas_call | solution.py:241
  117.2 1.7 %copy.10 = bf16[384,160]{0,1:T(8,128)(2,1)} copy(bf16[384,160]{1,0:T(8,128)(2,1)} %get-tuple-element.3) | data formatting | bytes 245760 | tf_op jit(solution)/shard_map/attend_and_project/pallas_call | solution.py:241

commit v2 on v1

v2 whole, which is shorter than its diff:
```python
import functools

import jax
import jax.numpy as jnp
from jax import lax
from jax.experimental import pallas as pl
from jax.experimental.pallas import tpu as pltpu
from jax.sharding import PartitionSpec as P

MESH = pl.DeviceIdType.MESH
HD = 128
F32 = jnp.float32
BF16 = jnp.bfloat16
DIMS = (4, 4, 4, 4, 2)


def nt_dot(a, b):
    return lax.dot_general(a, b, (((1,), (1,)), ((), ())), preferred_element_type=F32)


def kernel(
    dims, chunks,
    q_ref, k_ref, v_ref, dq_ref, dk_ref, dv_ref, w_ref,
    out_ref, dout_ref,
    qd_all, kd_all, v_in, vt_own, vt_all, w_in, wt_own, wt_all,
    part, stats, part_in, stats_in, mix, x_all, send_z, recv_z, hold_a, hold_b, own, swap_out, swap_in,
    q_s, q_r, k_s, k_r, v_s, v_r, w_s, w_r, p_s, p_r, t_s, t_r, x_s, x_r, z_s, z_r, c_s, c_r, l_s,
):
    nx, nz, ny, nh, nc = dims
    tok = q_ref.shape[0]
    col = out_ref.shape[1]
    scale = 1.0 / HD**0.5
    rate = scale * 1.4426950408889634

    ctx = lax.axis_index("ctx")
    fsdp = lax.axis_index("fsdp")
    zl, x = ctx // nx, lax.rem(ctx, nx)
    core = lax.rem(fsdp, nc)
    zh = lax.rem(fsdp // nc, nh)
    y = fsdp // (nc * nh)

    def at_x(d):
        return (zl * nx + lax.rem(x + d, nx), fsdp)

    def at_zl(d):
        return (lax.rem(zl + d, nz) * nx + x, fsdp)

    def at_zh(d):
        return (ctx, (y * nh + lax.rem(zh + d, nh)) * nc + core)

    def at_yc(e):
        return (ctx, (lax.rem(y + e // nc, ny) * nh + zh) * nc + lax.rem(core + e % nc, nc))

    partners = (
        [at_x(d) for d in range(1, nx)]
        + [at_zl(d) for d in range(1, nz)]
        + [at_zh(1), at_zh(nh - 1)]
        + [at_yc(e) for e in range(1, ny * nc)]
    )
    barrier = pltpu.get_barrier_semaphore()
    for device in partners:
        pl.semaphore_signal(barrier, inc=1, device_id=device, device_id_type=MESH)

    def remote(src, dst, s, r, device):
        return pltpu.make_async_remote_copy(
            src_ref=src, dst_ref=dst, send_sem=s, recv_sem=r, device_id=device, device_id_type=MESH
        )

    key_rows = pl.ds(pl.multiple_of(x * tok, tok), tok)
    first, second = slice(0, HD), slice(HD, 2 * HD)
    local = [
        pltpu.make_async_copy(src, dst, l_s.at[i])
        for i, (src, dst) in enumerate(
            [
                (v_ref, v_in.at[0]),
                (dv_ref, v_in.at[1]),
                (dq_ref, qd_all.at[zl, :, first]),
                (q_ref, qd_all.at[zl, :, second]),
                (k_ref, kd_all.at[key_rows, first]),
                (dk_ref, kd_all.at[key_rows, second]),
                (w_ref, w_in),
            ]
        )
    ]
    for copy in local:
        copy.start()
    for copy in local[:2]:
        copy.wait()
    vt_own[first, :] = v_in[0].T
    vt_own[second, :] = v_in[1].T
    for copy in local[2:6]:
        copy.wait()

    pl.semaphore_wait(barrier, len(partners))

    q_copies = [
        remote(qd_all.at[zl], qd_all.at[zl], q_s.at[d - 1], q_r.at[d - 1], at_zl(d))
        for d in range(1, nz)
    ]
    k_copies = [
        remote(kd_all.at[key_rows], kd_all.at[key_rows], k_s.at[d - 1], k_r.at[d - 1], at_x(d))
        for d in range(1, nx)
    ]
    v_copies = [
        remote(vt_own, vt_all.at[:, key_rows], v_s.at[d - 1], v_r.at[d - 1], at_x(d))
        for d in range(1, nx)
    ]
    for copy in q_copies + k_copies + v_copies:
        copy.start()
    v_local = pltpu.make_async_copy(vt_own, vt_all.at[:, key_rows], l_s.at[0])
    v_local.start()

    group = nh * nc * col
    local[6].wait()
    for i in range(ny):
        wt_own[i * group : (i + 1) * group, :] = w_in[:, i * group : (i + 1) * group].T
    slot = y * nc + core
    slot_cols = pl.ds(pl.multiple_of(slot * HD, HD), HD)

    def weight_rows(row):
        return pl.ds(pl.multiple_of(row * group, group), group)

    w_copies = [
        remote(
            wt_own.at[weight_rows(lax.rem(y + e // nc, ny))],
            wt_all.at[:, slot_cols],
            w_s.at[e - 1],
            w_r.at[e - 1],
            at_yc(e),
        )
        for e in range(1, ny * nc)
    ]
    for copy in w_copies:
        copy.start()
    w_local = pltpu.make_async_copy(wt_own.at[weight_rows(y)], wt_all.at[:, slot_cols], l_s.at[1])
    w_local.start()

    for copy in q_copies + k_copies + v_copies:
        copy.wait()
    v_local.wait()

    def part_copies(c, lanes, j, device):
        i = c * (nz - 1) + j
        return (
            remote(part.at[j, :, lanes], part_in.at[j, :, lanes], p_s.at[i], p_r.at[i], device),
            remote(stats.at[j, :, lanes], stats_in.at[j, :, lanes], t_s.at[i], t_r.at[i], device),
        )

    for c, (at, size) in enumerate(chunks):
        lanes = slice(at, at + size)

        def attend(j, carry):
            owner = lax.rem(zl + j + 1, nz)
            qd = qd_all[owner, lanes, :]
            scores = nt_dot(kd_all[:, first], qd[:, second])
            steps = nt_dot(kd_all[...], qd)
            top = jnp.max(scores, axis=0, keepdims=True)
            weights = jnp.exp2((scores - top) * rate)
            spread = weights * steps
            total = jnp.sum(weights, axis=0, keepdims=True)
            mean = jnp.sum(spread, axis=0, keepdims=True) * scale / total
            low = weights.astype(BF16)
            one = jnp.dot(vt_all[...], low, preferred_element_type=F32)
            two = jnp.dot(vt_all[first, :], spread.astype(BF16), preferred_element_type=F32)
            mixed = one[first] / total
            part[j, first, lanes] = mixed.astype(BF16)
            part[j, second, lanes] = ((one[second] + two * scale) / total - mean * mixed).astype(
                BF16
            )
            stats[j, 0:1, lanes] = top * rate
            stats[j, 1:2, lanes] = total
            stats[j, 2:3, lanes] = mean
            stats[j, 3:8, lanes] = jnp.zeros((5, size), F32)

            @pl.when(j < nz - 1)
            def _():
                for copy in part_copies(c, lanes, j, (owner * nx + x, fsdp)):
                    copy.start()

            return carry

        lax.fori_loop(0, nz, attend, 0)

    block = nc * col
    slot_rows = pl.ds(pl.multiple_of(slot * HD, HD), HD)
    top_half, low_half = slice(0, block // 2), slice(block // 2, block)
    other = lax.rem(core + 1, nc)

    def merge(c):
        at, size = chunks[c]
        lanes = slice(at, at + size)
        for j in range(nz - 1):
            for copy in part_copies(c, lanes, j, at_zl(j + 1)):
                copy.wait()
        parts = [(part_in.at[j], stats_in.at[j]) for j in range(nz - 1)]
        parts.append((part.at[nz - 1], stats.at[nz - 1]))
        tops = [s[0:1, lanes] for _, s in parts]
        top = functools.reduce(jnp.maximum, tops)
        shares = [jnp.exp2(t - top) * s[1:2, lanes] for t, (_, s) in zip(tops, parts)]
        total = sum(shares)
        shares = [s / total for s in shares]
        means = [s[2:3, lanes] for _, s in parts]
        mean = sum(a * b for a, b in zip(shares, means))
        mixed = jnp.zeros((HD, size), F32)
        tangent = jnp.zeros((HD, size), F32)
        for share, here, (p, _) in zip(shares, means, parts):
            one = p[first, lanes].astype(F32)
            mixed += share * one
            tangent += share * (p[second, lanes].astype(F32) + (here - mean) * one)
        mix[0, :, lanes] = mixed.astype(BF16)
        mix[1, :, lanes] = tangent.astype(BF16)
        n = ny * nc - 1
        copies = [
            remote(
                mix.at[lax.rem(core + e % nc, nc), :, lanes],
                x_all.at[slot_rows, lanes],
                x_s.at[c * n + e - 1],
                x_r.at[c * n + e - 1],
                at_yc(e),
            )
            for e in range(1, ny * nc)
        ]
        for copy in copies:
            copy.start()
        x_all[slot_rows, lanes] = mix[core, :, lanes]
        return copies

    def z_copy(c, i, d):
        at, size = chunks[c]
        lanes = slice(at, at + size)
        k = 6 * c + i
        return remote(
            send_z.at[i, :, lanes], recv_z.at[i, :, lanes], z_s.at[k], z_r.at[k], at_zh(d)
        )

    def project(c):
        at, size = chunks[c]
        lanes = slice(at, at + size)

        def dot(d):
            rows = pl.ds(pl.multiple_of(lax.rem(zh + d, nh) * block, block), block)
            return jnp.dot(wt_all[rows, :], x_all[:, lanes], preferred_element_type=F32)

        far = dot(2)
        send_z[0, :, lanes] = far[top_half].astype(BF16)
        send_z[1, :, lanes] = far[low_half].astype(BF16)
        copies = [z_copy(c, 0, 1), z_copy(c, 1, 3)]
        for copy in copies:
            copy.start()
        after = dot(1)
        hold_a[:, lanes] = after[top_half]
        send_z[2, :, lanes] = after[low_half].astype(BF16)
        copies.append(z_copy(c, 2, 1))
        copies[2].start()
        before = dot(3)
        hold_b[:, lanes] = before[low_half]
        send_z[3, :, lanes] = before[top_half].astype(BF16)
        copies.append(z_copy(c, 3, 3))
        copies[3].start()
        own[:, lanes] = dot(0)
        return copies

    def forward(c, copies):
        at, size = chunks[c]
        lanes = slice(at, at + size)
        for i, hold, d in ((0, hold_a, 1), (1, hold_b, 3)):
            copies[i].wait()
            send_z[4 + i, :, lanes] = (hold[:, lanes] + recv_z[i, :, lanes].astype(F32)).astype(
                BF16
            )
            copies.append(z_copy(c, 4 + i, d))
            copies[4 + i].start()

    def cols(i):
        return pl.ds(pl.multiple_of(i * col, col), col)

    def finish(c, copies):
        at, size = chunks[c]
        lanes = slice(at, at + size)
        for copy in copies[2:]:
            copy.wait()
        for rows, i, j in ((top_half, 3, 4), (low_half, 2, 5)):
            total = own[rows, lanes] + recv_z[i, :, lanes].astype(F32)
            swap_out[rows, lanes] = (total + recv_z[j, :, lanes].astype(F32)).astype(BF16)
        copy = remote(
            swap_out.at[cols(other), lanes], swap_in.at[:, lanes], c_s.at[c], c_r.at[c], at_yc(1)
        )
        copy.start()
        return copy

    def write(c, copy):
        at, size = chunks[c]
        lanes = slice(at, at + size)
        mine = swap_out[cols(core), lanes]
        copy.wait()
        theirs = swap_in[:, lanes]
        out_ref[lanes, :] = jnp.where(core == 0, mine, theirs).T
        dout_ref[lanes, :] = jnp.where(core == 0, theirs, mine).T

    last = len(chunks) - 1
    sends = {}
    for c in range(last + 1):
        x_copies = merge(c)
        if c > 0:
            forward(c - 1, sends[c - 1])
        if c == 0:
            for copy in w_copies:
                copy.wait()
            w_local.wait()
        for copy in x_copies:
            copy.wait()
        sends[c] = project(c)
    swaps = {c: finish(c, sends[c]) for c in range(last)}
    forward(last, sends[last])
    for c in range(last):
        write(c, swaps[c])
    write(last, finish(last, sends[last]))


def call(dims, q, k, v, dq, dk, dv, w):
    nx, nz, ny, nh, nc = dims
    tok = q.shape[0]
    col = w.shape[1] // (ny * nh * nc)
    block = nc * col
    group = nh * block
    peers = ny * nc
    chunks = ((0, HD), (HD, tok - HD))
    n = len(chunks)
    dma = pltpu.SemaphoreType.DMA
    vmem = pl.BlockSpec(memory_space=pltpu.VMEM)

    def pair(n):
        return [dma((max(n, 1),)), dma((max(n, 1),))]

    return pl.pallas_call(
        functools.partial(kernel, dims, chunks),
        out_shape=(
            jax.ShapeDtypeStruct((tok, col), BF16),
            jax.ShapeDtypeStruct((tok, col), BF16),
        ),
        in_specs=[pl.BlockSpec(memory_space=pl.ANY)] * 7,
        out_specs=(vmem, vmem),
        scratch_shapes=[
            pltpu.VMEM((nz, tok, 2 * HD), BF16),
            pltpu.VMEM((nx * tok, 2 * HD), BF16),
            pltpu.VMEM((2, tok, HD), BF16),
            pltpu.VMEM((2 * HD, tok), BF16),
            pltpu.VMEM((2 * HD, nx * tok), BF16),
            pltpu.VMEM(w.shape, BF16),
            pltpu.VMEM((w.shape[1], HD), BF16),
            pltpu.VMEM((group, peers * HD), BF16),
            pltpu.VMEM((nz, 2 * HD, tok), BF16),
            pltpu.VMEM((nz, 8, tok), F32),
            pltpu.VMEM((max(nz - 1, 1), 2 * HD, tok), BF16),
            pltpu.VMEM((max(nz - 1, 1), 8, tok), F32),
            pltpu.VMEM((2, HD, tok), BF16),
            pltpu.VMEM((peers * HD, tok), BF16),
            pltpu.VMEM((6, block // 2, tok), BF16),
            pltpu.VMEM((6, block // 2, tok), BF16),
            pltpu.VMEM((block // 2, tok), F32),
            pltpu.VMEM((block // 2, tok), F32),
            pltpu.VMEM((block, tok), F32),
            pltpu.VMEM((block, tok), BF16),
            pltpu.VMEM((col, tok), BF16),
        ]
        + pair(nz - 1)
        + pair(nx - 1)
        + pair(nx - 1)
        + pair(peers - 1)
        + pair(n * (nz - 1))
        + pair(n * (nz - 1))
        + pair(n * (peers - 1))
        + pair(n * 6)
        + pair(n)
        + [dma((7,))],
        compiler_params=pltpu.CompilerParams(
            collective_id=0, has_side_effects=True, vmem_limit_bytes=56 * 1024 * 1024
        ),
        name="attend_and_project",
    )(q, k, v, dq, dk, dv, w)


def solution(mesh, dims=DIMS):
    spec = P("ctx", "fsdp")
    return jax.shard_map(
        functools.partial(call, dims),
        mesh=mesh,
        in_specs=(spec,) * 6 + (P("fsdp", None),),
        out_specs=(spec, spec),
        check_vma=False,
    )
```

time: 119 us -> 98 us (0.82)
  the two profiles are of different devices: /device:TPU:33 before, /device:TPU:35 now
where the time goes in v2:
time: 98 us; the launch traced here: 97.9 us
  Pallas kernels  93.8 us (96%)
  local copies, waits for them, and re-layouts  3.38 us (3%)
    pallas_call x1, Pallas kernels, call(): pl.pallas_call(functools.partial(kernel, dims, chunks), out_shape=(jax.Sh...  93.8 us
    pallas_call x2, local copies, waits for them, and re-layouts, call(): pl.pallas_call(functools.partial(kernel, dims, chunks), out_shape=(jax.Sh...  3.38 us

profile of v2, /device:TPU:35, one launch (start us, length us, event | category | flops | bytes accessed | tf_op | source)
XLA Modules:
  0.0 97.9 jit_solution(13566410286783882002)
XLA Ops:
  0.6 93.8 %attend_and_project.1 = (bf16[384,160]{1,0:T(8,128)(2,1)}, bf16[384,160]{1,0:T(8,128)(2,1)}) custom-call(bf16[384,128]{1,0:T(8,128)(2,1)} %q_ref.1, bf16[384,128]{1,0:T(8,128)(2,1)} %k_ref.1, bf16[384,128]{1,0:T(8,128)(2,1)} %v_ref.1, bf16[384,128]{1,0:T(8,128)(2,1)} %dq_ref.1, bf16[384,128]{1,0:T(8,128)(2,1)} %dk_ref.1, bf16[384,128]{1,0:T(8,128)(2,1)} %dv_ref.1, ...), custom_call_target="tpu_custom_call" | custom-call | tf_op jit(solution)/shard_map/attend_and_project/pallas_call | solution.py:335
  94.5 1.7 %copy.9 = bf16[384,160]{0,1:T(8,128)(2,1)} copy(bf16[384,160]{1,0:T(8,128)(2,1)} %get-tuple-element.2) | data formatting | bytes 245760 | tf_op jit(solution)/shard_map/attend_and_project/pallas_call | solution.py:335
  96.2 1.7 %copy.10 = bf16[384,160]{0,1:T(8,128)(2,1)} copy(bf16[384,160]{1,0:T(8,128)(2,1)} %get-tuple-element.3) | data formatting | bytes 245760 | tf_op jit(solution)/shard_map/attend_and_project/pallas_call | solution.py:335

commit v3 on v2

--- a/solution.py
+++ b/solution.py
@@ -28,7 +28,7 @@
 ):
     nx, nz, ny, nh, nc = dims
     tok = q_ref.shape[0]
-    col = out_ref.shape[1]
+    col = out_ref.shape[0]
     scale = 1.0 / HD**0.5
     rate = scale * 1.4426950408889634
 
@@ -52,9 +52,9 @@
         return (ctx, (lax.rem(y + e // nc, ny) * nh + zh) * nc + lax.rem(core + e % nc, nc))
 
     partners = (
-        [at_x(d) for d in range(1, nx)]
+        ([at_x(1), at_x(nx - 1)] if nx > 1 else [])
         + [at_zl(d) for d in range(1, nz)]
-        + [at_zh(1), at_zh(nh - 1)]
+        + ([at_zh(1), at_zh(nh - 1)] if nh > 1 else [])
         + [at_yc(e) for e in range(1, ny * nc)]
     )
     barrier = pltpu.get_barrier_semaphore()
@@ -93,19 +93,47 @@
 
     pl.semaphore_wait(barrier, len(partners))
 
-    q_copies = [
-        remote(qd_all.at[zl], qd_all.at[zl], q_s.at[d - 1], q_r.at[d - 1], at_zl(d))
-        for d in range(1, nz)
-    ]
-    k_copies = [
-        remote(kd_all.at[key_rows], kd_all.at[key_rows], k_s.at[d - 1], k_r.at[d - 1], at_x(d))
-        for d in range(1, nx)
-    ]
-    v_copies = [
-        remote(vt_own, vt_all.at[:, key_rows], v_s.at[d - 1], v_r.at[d - 1], at_x(d))
-        for d in range(1, nx)
-    ]
-    for copy in q_copies + k_copies + v_copies:
+    def q_copy(d, i):
+        return remote(qd_all.at[zl], qd_all.at[zl], q_s.at[i], q_r.at[i], at_zl(d))
+
+    def q_relay(d, i):
+        there = lax.rem(zl + 2, nz)
+        return remote(qd_all.at[there], qd_all.at[there], q_s.at[3], q_r.at[i], at_zl(d))
+
+    def rows_of(d):
+        return pl.ds(pl.multiple_of(lax.rem(x + d, nx) * tok, tok), tok)
+
+    def k_copy(i, d, rows):
+        return remote(kd_all.at[rows], kd_all.at[rows], k_s.at[i], k_r.at[i], at_x(d))
+
+    def v_copy(i, d):
+        return remote(vt_own, vt_all.at[:, key_rows], v_s.at[i], v_r.at[i], at_x(d))
+
+    def v_relay(i, d, rows):
+        return remote(vt_all.at[:, rows], vt_all.at[:, rows], v_s.at[i], v_r.at[i], at_x(d))
+
+    x_way = []
+    if nx > 1:
+        x_way = [
+            k_copy(0, 1, key_rows),
+            v_copy(1, nx - 1),
+            v_copy(0, 1),
+            k_copy(1, nx - 1, key_rows),
+        ]
+        for copy in x_way[:2]:
+            copy.start()
+    if nz > 1:
+        q_copy(2, 1).start()
+
+        @pl.when(zl != nz - 1)
+        def _():
+            q_copy(1, 0).start()
+
+        @pl.when(zl != 0)
+        def _():
+            q_copy(3, 2).start()
+
+    for copy in x_way[2:]:
         copy.start()
     v_local = pltpu.make_async_copy(vt_own, vt_all.at[:, key_rows], l_s.at[0])
     v_local.start()
@@ -120,24 +148,64 @@
     def weight_rows(row):
         return pl.ds(pl.multiple_of(row * group, group), group)
 
-    w_copies = [
-        remote(
-            wt_own.at[weight_rows(lax.rem(y + e // nc, ny))],
+    def w_copy(d):
+        return remote(
+            wt_own.at[weight_rows(lax.rem(y + d, ny))],
             wt_all.at[:, slot_cols],
-            w_s.at[e - 1],
-            w_r.at[e - 1],
-            at_yc(e),
-        )
-        for e in range(1, ny * nc)
-    ]
+            w_s.at[d],
+            w_r.at[d],
+            at_yc(d * nc) if d else at_yc(1),
+        )
+
+    def w_relay(d):
+        there = pl.ds(pl.multiple_of((lax.rem(y + ny - d, ny) * nc + core) * HD, HD), HD)
+        i = ny + d - 1
+        return remote(wt_all.at[:, there], wt_all.at[:, there], w_s.at[i], w_r.at[i], at_yc(1))
+
+    w_copies = [w_copy(d) for d in list(range(1, ny)) + [0]]
     for copy in w_copies:
         copy.start()
     w_local = pltpu.make_async_copy(wt_own.at[weight_rows(y)], wt_all.at[:, slot_cols], l_s.at[1])
     w_local.start()
 
-    for copy in q_copies + k_copies + v_copies:
+    if nx > 1:
+        x_way[0].wait_recv()
+        x_way.append(k_copy(2, 1, rows_of(nx - 1)))
+        x_way[4].start()
+        x_way[1].wait_recv()
+        x_way.append(v_relay(2, nx - 1, rows_of(1)))
+        x_way[5].start()
+    if nz > 1:
+        q_copy(2, 1).wait()
+
+        @pl.when(zl == 2)
+        def _():
+            q_relay(1, 2).start()
+
+        @pl.when(zl == 1)
+        def _():
+            q_relay(3, 0).start()
+
+    for copy in x_way[:2]:
+        copy.wait_send()
+    for copy in x_way[2:]:
         copy.wait()
     v_local.wait()
+    if nz > 1:
+        for d in (1, 3):
+            q_copy(d, d - 1).wait_recv()
+
+        @pl.when(zl != nz - 1)
+        def _():
+            q_copy(1, 0).wait_send()
+
+        @pl.when(zl != 0)
+        def _():
+            q_copy(3, 2).wait_send()
+
+        @pl.when(lax.rem(zl, nz - 1) != 0)
+        def _():
+            q_relay(1, 2).wait_send()
 
     def part_copies(c, lanes, j, device):
         i = c * (nz - 1) + j
@@ -180,6 +248,13 @@
             return carry
 
         lax.fori_loop(0, nz, attend, 0)
+        if c == 0:
+            for copy in w_copies:
+                copy.wait()
+            relays = [w_relay(d) for d in range(1, ny)]
+            for copy in relays:
+                copy.start()
+            w_copies = relays
 
     block = nc * col
     slot_rows = pl.ds(pl.multiple_of(slot * HD, HD), HD)
@@ -241,6 +316,9 @@
             rows = pl.ds(pl.multiple_of(lax.rem(zh + d, nh) * block, block), block)
             return jnp.dot(wt_all[rows, :], x_all[:, lanes], preferred_element_type=F32)
 
+        own[:, lanes] = dot(0)
+        if nh == 1:
+            return []
         far = dot(2)
         send_z[0, :, lanes] = far[top_half].astype(BF16)
         send_z[1, :, lanes] = far[low_half].astype(BF16)
@@ -257,13 +335,12 @@
         send_z[3, :, lanes] = before[top_half].astype(BF16)
         copies.append(z_copy(c, 3, 3))
         copies[3].start()
-        own[:, lanes] = dot(0)
         return copies
 
     def forward(c, copies):
         at, size = chunks[c]
         lanes = slice(at, at + size)
-        for i, hold, d in ((0, hold_a, 1), (1, hold_b, 3)):
+        for i, hold, d in ((0, hold_a, 1), (1, hold_b, 3)) if nh > 1 else ():
             copies[i].wait()
             send_z[4 + i, :, lanes] = (hold[:, lanes] + recv_z[i, :, lanes].astype(F32)).astype(
                 BF16
@@ -280,8 +357,10 @@
         for copy in copies[2:]:
             copy.wait()
         for rows, i, j in ((top_half, 3, 4), (low_half, 2, 5)):
-            total = own[rows, lanes] + recv_z[i, :, lanes].astype(F32)
-            swap_out[rows, lanes] = (total + recv_z[j, :, lanes].astype(F32)).astype(BF16)
+            total = own[rows, lanes]
+            if nh > 1:
+                total += recv_z[i, :, lanes].astype(F32) + recv_z[j, :, lanes].astype(F32)
+            swap_out[rows, lanes] = total.astype(BF16)
         copy = remote(
             swap_out.at[cols(other), lanes], swap_in.at[:, lanes], c_s.at[c], c_r.at[c], at_yc(1)
         )
@@ -294,8 +373,8 @@
         mine = swap_out[cols(core), lanes]
         copy.wait()
         theirs = swap_in[:, lanes]
-        out_ref[lanes, :] = jnp.where(core == 0, mine, theirs).T
-        dout_ref[lanes, :] = jnp.where(core == 0, theirs, mine).T
+        out_ref[:, lanes] = jnp.where(core == 0, mine, theirs)
+        dout_ref[:, lanes] = jnp.where(core == 0, theirs, mine)
 
     last = len(chunks) - 1
     sends = {}
@@ -317,6 +396,11 @@
     write(last, finish(last, sends[last]))
 
 
+def hand_over(a_ref, b_ref, out_ref, dout_ref):
+    out_ref[...] = a_ref[...]
+    dout_ref[...] = b_ref[...]
+
+
 def call(dims, q, k, v, dq, dk, dv, w):
     nx, nz, ny, nh, nc = dims
     tok = q.shape[0]
@@ -332,12 +416,10 @@
     def pair(n):
         return [dma((max(n, 1),)), dma((max(n, 1),))]
 
-    return pl.pallas_call(
+    out = jax.ShapeDtypeStruct((col, tok), BF16)
+    results = pl.pallas_call(
         functools.partial(kernel, dims, chunks),
-        out_shape=(
-            jax.ShapeDtypeStruct((tok, col), BF16),
-            jax.ShapeDtypeStruct((tok, col), BF16),
-        ),
+        out_shape=(out, out),
         in_specs=[pl.BlockSpec(memory_space=pl.ANY)] * 7,
         out_specs=(vmem, vmem),
         scratch_shapes=[
@@ -363,10 +445,10 @@
             pltpu.VMEM((block, tok), BF16),
             pltpu.VMEM((col, tok), BF16),
         ]
-        + pair(nz - 1)
-        + pair(nx - 1)
-        + pair(nx - 1)
-        + pair(peers - 1)
+        + pair(4)
+        + pair(3)
+        + pair(3)
+        + pair(2 * ny - 1)
         + pair(n * (nz - 1))
         + pair(n * (nz - 1))
         + pair(n * (peers - 1))
@@ -378,6 +460,14 @@
         ),
         name="attend_and_project",
     )(q, k, v, dq, dk, dv, w)
+    results = pl.pallas_call(
+        hand_over,
+        out_shape=(out, out),
+        in_specs=[vmem, vmem],
+        out_specs=(vmem, vmem),
+        name="hand_over",
+    )(*results)
+    return tuple(r.T for r in results)
 
 
 def solution(mesh, dims=DIMS):

time: 98 us -> 91 us (0.929)
  the two profiles are of different devices: /device:TPU:35 before, /device:TPU:97 now
where the time goes in v3:
time: 91 us; the launch traced here: 90.9 us
  Pallas kernels  90.2 us (99%)
    pallas_call x1, Pallas kernels, call(): pl.pallas_call(functools.partial(kernel, dims, chunks), out_shape=(out, o...  88.6 us

profile of v3, /device:TPU:97, one launch (start us, length us, event | category | flops | bytes accessed | tf_op | source)
XLA Modules:
  0.0 90.9 jit_solution(14242027942194734903)
XLA Ops:
  0.6 88.6 %attend_and_project.1 = (bf16[160,384]{1,0:T(8,128)(2,1)}, bf16[160,384]{1,0:T(8,128)(2,1)}) custom-call(bf16[384,128]{1,0:T(8,128)(2,1)} %q_ref.1, bf16[384,128]{1,0:T(8,128)(2,1)} %k_ref.1, bf16[384,128]{1,0:T(8,128)(2,1)} %v_ref.1, bf16[384,128]{1,0:T(8,128)(2,1)} %dq_ref.1, bf16[384,128]{1,0:T(8,128)(2,1)} %dk_ref.1, bf16[384,128]{1,0:T(8,128)(2,1)} %dv_ref.1, ...), custom_call_target="tpu_custom_call" | custom-call | tf_op jit(solution)/shard_map/attend_and_project/pallas_call | solution.py:420
  89.2 1.7 %hand_over.1 = (bf16[160,384]{1,0:T(8,128)(2,1)}, bf16[160,384]{1,0:T(8,128)(2,1)}) custom-call(bf16[160,384]{1,0:T(8,128)(2,1)} %get-tuple-element.6.a_ref, bf16[160,384]{1,0:T(8,128)(2,1)} %get-tuple-element.7.b_ref), custom_call_target="tpu_custom_call" | custom-call | tf_op jit(solution)/shard_map/hand_over/pallas_call | solution.py:463

commit v4 on v3

--- a/solution.py
+++ b/solution.py
@@ -23,8 +23,8 @@
     q_ref, k_ref, v_ref, dq_ref, dk_ref, dv_ref, w_ref,
     out_ref, dout_ref,
     qd_all, kd_all, v_in, vt_own, vt_all, w_in, wt_own, wt_all,
-    part, stats, part_in, stats_in, mix, x_all, send_z, recv_z, hold_a, hold_b, own, swap_out, swap_in,
-    q_s, q_r, k_s, k_r, v_s, v_r, w_s, w_r, p_s, p_r, t_s, t_r, x_s, x_r, z_s, z_r, c_s, c_r, l_s,
+    part, stats, part_in, stats_in, via_in, via_stats, mix, x_all, send_z, recv_z, hold_a, hold_b, own, swap_out, swap_in,
+    q_s, q_r, k_s, k_r, v_s, v_r, w_s, w_r, p_s, p_r, t_s, t_r, u_r, x_s, x_r, z_s, z_r, c_s, c_r, l_s,
 ):
     nx, nz, ny, nh, nc = dims
     tok = q_ref.shape[0]
@@ -207,54 +207,108 @@
         def _():
             q_relay(1, 2).wait_send()
 
-    def part_copies(c, lanes, j, device):
-        i = c * (nz - 1) + j
+    def part_copies(c, owner, device):
+        i, k = c * nz + owner, c * nz + zl
         return (
-            remote(part.at[j, :, lanes], part_in.at[j, :, lanes], p_s.at[i], p_r.at[i], device),
-            remote(stats.at[j, :, lanes], stats_in.at[j, :, lanes], t_s.at[i], t_r.at[i], device),
+            remote(part[c].at[owner], part_in[c].at[zl], p_s.at[i], p_r.at[k], device),
+            remote(stats[c].at[owner], stats_in[c].at[zl], t_s.at[i], t_r.at[k], device),
         )
 
-    for c, (at, size) in enumerate(chunks):
-        lanes = slice(at, at + size)
-
-        def attend(j, carry):
-            owner = lax.rem(zl + j + 1, nz)
-            qd = qd_all[owner, lanes, :]
-            scores = nt_dot(kd_all[:, first], qd[:, second])
-            steps = nt_dot(kd_all[...], qd)
-            top = jnp.max(scores, axis=0, keepdims=True)
-            weights = jnp.exp2((scores - top) * rate)
-            spread = weights * steps
-            total = jnp.sum(weights, axis=0, keepdims=True)
-            mean = jnp.sum(spread, axis=0, keepdims=True) * scale / total
-            low = weights.astype(BF16)
-            one = jnp.dot(vt_all[...], low, preferred_element_type=F32)
-            two = jnp.dot(vt_all[first, :], spread.astype(BF16), preferred_element_type=F32)
-            mixed = one[first] / total
-            part[j, first, lanes] = mixed.astype(BF16)
-            part[j, second, lanes] = ((one[second] + two * scale) / total - mean * mixed).astype(
-                BF16
+    def via_copies(c, owner, device):
+        i = c * nz + owner
+        return (
+            remote(part[c].at[owner], via_in[c], p_s.at[i], u_r.at[c], device),
+            remote(stats[c].at[owner], via_stats[c], t_s.at[i], u_r.at[len(chunks) + c], device),
+        )
+
+    def combine(parts):
+        tops = [s[0:1, :] for _, s in parts]
+        top = functools.reduce(jnp.maximum, tops)
+        shares = [jnp.exp2(t - top) * s[1:2, :] for t, (_, s) in zip(tops, parts)]
+        total = sum(shares)
+        shares = [s / total for s in shares]
+        means = [s[2:3, :] for _, s in parts]
+        mean = sum(a * b for a, b in zip(shares, means))
+        mixed = tangent = None
+        for share, here, (p, _) in zip(shares, means, parts):
+            one = p[first, :].astype(F32)
+            two = p[second, :].astype(F32) + (here - mean) * one
+            mixed = share * one if mixed is None else mixed + share * one
+            tangent = share * two if tangent is None else tangent + share * two
+        return mixed, tangent, top, total, mean
+
+    at_end = lax.rem(zl, nz - 1) == 0 if nz > 1 else True
+    if nz > 1:
+
+        @pl.when(at_end)
+        def _():
+            for c in range(len(chunks)):
+                part_in[c][nz - 1 - zl] = jnp.zeros_like(part_in[c][0])
+                stats_in[c][nz - 1 - zl] = jnp.zeros_like(stats_in[c][0])
+                stats_in[c][nz - 1 - zl, 0:1, :] = jnp.full_like(stats_in[c][0, 0:1, :], -1e30)
+
+    order = (27 + 87 * ((zl + 1) // 2) + 27 * (zl // 2)) if nz > 1 else 0
+
+    owners = [lax.rem(order // 4**j, 4) for j in range(nz)]
+
+    def attend(c, begin, end):
+        at, size = chunks[c]
+        mine = owners[begin:end]
+        qd = jnp.concatenate([qd_all[owner, at : at + size, :] for owner in mine], axis=0)
+        scores = nt_dot(kd_all[:, first], qd[:, second])
+        steps = nt_dot(kd_all[...], qd)
+        top = jnp.max(scores, axis=0, keepdims=True)
+        weights = jnp.exp2((scores - top) * rate)
+        spread = weights * steps
+        total = jnp.sum(weights, axis=0, keepdims=True)
+        mean = jnp.sum(spread, axis=0, keepdims=True) * scale / total
+        low = weights.astype(BF16)
+        one = jnp.dot(vt_all[...], low, preferred_element_type=F32)
+        two = jnp.dot(vt_all[first, :], spread.astype(BF16), preferred_element_type=F32)
+        mixed = one[first] / total
+        tangent = (one[second] + two * scale) / total - mean * mixed
+        for i, owner in enumerate(mine):
+            lanes = slice(i * size, (i + 1) * size)
+            part[c][owner, first, :] = mixed[:, lanes].astype(BF16)
+            part[c][owner, second, :] = tangent[:, lanes].astype(BF16)
+            stats[c][owner, 0:1, :] = top[:, lanes] * rate
+            stats[c][owner, 1:2, :] = total[:, lanes]
+            stats[c][owner, 2:3, :] = mean[:, lanes]
+            stats[c][owner, 3:8, :] = jnp.zeros((5, size), F32)
+        for j in range(begin, min(end, nz - 1)):
+            owner = owners[j]
+
+            @pl.when(at_end if j == 2 else jnp.logical_not(at_end) if j == 0 else j == 1)
+            def _():
+                for copy in part_copies(c, owner, (owner * nx + x, fsdp)):
+                    copy.start()
+
+            if j == 0:
+
+                @pl.when(at_end)
+                def _():
+                    for copy in via_copies(c, owner, ((1 + zl // 3) * nx + x, fsdp)):
+                        copy.start()
+
+    def merge_on_way(c):
+        if nz == 1:
+            return
+
+        @pl.when(jnp.logical_not(at_end))
+        def _():
+            far = owners[2]
+            for copy in via_copies(c, far, (far * nx + x, fsdp)):
+                copy.wait_recv()
+            mixed, tangent, top, total, mean = combine(
+                [(part[c].at[far], stats[c].at[far]), (via_in[c], via_stats[c])]
             )
-            stats[j, 0:1, lanes] = top * rate
-            stats[j, 1:2, lanes] = total
-            stats[j, 2:3, lanes] = mean
-            stats[j, 3:8, lanes] = jnp.zeros((5, size), F32)
-
-            @pl.when(j < nz - 1)
-            def _():
-                for copy in part_copies(c, lanes, j, (owner * nx + x, fsdp)):
-                    copy.start()
-
-            return carry
-
-        lax.fori_loop(0, nz, attend, 0)
-        if c == 0:
-            for copy in w_copies:
-                copy.wait()
-            relays = [w_relay(d) for d in range(1, ny)]
-            for copy in relays:
+            part[c][far, first, :] = mixed.astype(BF16)
+            part[c][far, second, :] = tangent.astype(BF16)
+            stats[c][far, 0:1, :] = top
+            stats[c][far, 1:2, :] = total
+            stats[c][far, 2:3, :] = mean
+            for copy in part_copies(c, far, (far * nx + x, fsdp)):
                 copy.start()
-            w_copies = relays
 
     block = nc * col
     slot_rows = pl.ds(pl.multiple_of(slot * HD, HD), HD)
@@ -264,31 +318,32 @@
     def merge(c):
         at, size = chunks[c]
         lanes = slice(at, at + size)
-        for j in range(nz - 1):
-            for copy in part_copies(c, lanes, j, at_zl(j + 1)):
-                copy.wait()
-        parts = [(part_in.at[j], stats_in.at[j]) for j in range(nz - 1)]
-        parts.append((part.at[nz - 1], stats.at[nz - 1]))
-        tops = [s[0:1, lanes] for _, s in parts]
-        top = functools.reduce(jnp.maximum, tops)
-        shares = [jnp.exp2(t - top) * s[1:2, lanes] for t, (_, s) in zip(tops, parts)]
-        total = sum(shares)
-        shares = [s / total for s in shares]
-        means = [s[2:3, lanes] for _, s in parts]
-        mean = sum(a * b for a, b in zip(shares, means))
-        mixed = jnp.zeros((HD, size), F32)
-        tangent = jnp.zeros((HD, size), F32)
-        for share, here, (p, _) in zip(shares, means, parts):
-            one = p[first, lanes].astype(F32)
-            mixed += share * one
-            tangent += share * (p[second, lanes].astype(F32) + (here - mean) * one)
-        mix[0, :, lanes] = mixed.astype(BF16)
-        mix[1, :, lanes] = tangent.astype(BF16)
+        for d in range(1, nz):
+            there = lax.rem(zl + d, nz)
+            i = c * nz + there
+            device = at_zl(d)
+            copies = (
+                remote(part[c].at[there], part_in[c].at[there], p_s.at[i], p_r.at[i], device),
+                remote(stats[c].at[there], stats_in[c].at[there], t_s.at[i], t_r.at[i], device),
+            )
+            for copy in copies:
+                copy.wait_send()
+
+            @pl.when(jnp.logical_not(at_end) | (there != nz - 1 - zl))
+            def _():
+                for copy in copies:
+                    copy.wait_recv()
+
+        others = [lax.rem(zl + d, nz) for d in range(1, nz)]
+        parts = [(part_in[c].at[i], stats_in[c].at[i]) for i in others]
+        mixed, tangent, _, _, _ = combine(parts + [(part[c].at[zl], stats[c].at[zl])])
+        mix[c][0] = mixed.astype(BF16)
+        mix[c][1] = tangent.astype(BF16)
         n = ny * nc - 1
         copies = [
             remote(
-                mix.at[lax.rem(core + e % nc, nc), :, lanes],
-                x_all.at[slot_rows, lanes],
+                mix[c].at[lax.rem(core + e % nc, nc)],
+                x_all[c].at[slot_rows],
                 x_s.at[c * n + e - 1],
                 x_r.at[c * n + e - 1],
                 at_yc(e),
@@ -297,52 +352,48 @@
         ]
         for copy in copies:
             copy.start()
-        x_all[slot_rows, lanes] = mix[core, :, lanes]
+        x_all[c][slot_rows, :] = mix[c][core]
         return copies
 
     def z_copy(c, i, d):
-        at, size = chunks[c]
-        lanes = slice(at, at + size)
         k = 6 * c + i
-        return remote(
-            send_z.at[i, :, lanes], recv_z.at[i, :, lanes], z_s.at[k], z_r.at[k], at_zh(d)
-        )
+        return remote(send_z[c].at[i], recv_z[c].at[i], z_s.at[k], z_r.at[k], at_zh(d))
 
     def project(c):
-        at, size = chunks[c]
-        lanes = slice(at, at + size)
-
         def dot(d):
             rows = pl.ds(pl.multiple_of(lax.rem(zh + d, nh) * block, block), block)
-            return jnp.dot(wt_all[rows, :], x_all[:, lanes], preferred_element_type=F32)
-
-        own[:, lanes] = dot(0)
+            return jnp.dot(wt_all[rows, :], x_all[c][...], preferred_element_type=F32)
+
         if nh == 1:
+            own[c][...] = dot(0)
             return []
+        copies = [z_copy(c, i, d) for i, d in enumerate((1, 3, 1, 3))]
         far = dot(2)
-        send_z[0, :, lanes] = far[top_half].astype(BF16)
-        send_z[1, :, lanes] = far[low_half].astype(BF16)
-        copies = [z_copy(c, 0, 1), z_copy(c, 1, 3)]
-        for copy in copies:
+        send_z[c][0] = far[top_half].astype(BF16)
+        send_z[c][1] = far[low_half].astype(BF16)
+        after = dot(1)
+        hold_a[c][...] = after[top_half]
+        send_z[c][2] = after[low_half].astype(BF16)
+        before = dot(3)
+        hold_b[c][...] = before[low_half]
+        send_z[c][3] = before[top_half].astype(BF16)
+        own[c][...] = dot(0)
+        return copies
+
+    def send(copies):
+        for copy in copies[:2]:
             copy.start()
-        after = dot(1)
-        hold_a[:, lanes] = after[top_half]
-        send_z[2, :, lanes] = after[low_half].astype(BF16)
-        copies.append(z_copy(c, 2, 1))
-        copies[2].start()
-        before = dot(3)
-        hold_b[:, lanes] = before[low_half]
-        send_z[3, :, lanes] = before[top_half].astype(BF16)
-        copies.append(z_copy(c, 3, 3))
-        copies[3].start()
-        return copies
 
     def forward(c, copies):
         at, size = chunks[c]
         lanes = slice(at, at + size)
+        for copy in copies[:2]:
+            copy.wait_send()
+        for copy in copies[2:]:
+            copy.start()
         for i, hold, d in ((0, hold_a, 1), (1, hold_b, 3)) if nh > 1 else ():
-            copies[i].wait()
-            send_z[4 + i, :, lanes] = (hold[:, lanes] + recv_z[i, :, lanes].astype(F32)).astype(
+            copies[i].wait_recv()
+            send_z[c][4 + i] = (hold[c][...] + recv_z[c][i].astype(F32)).astype(
                 BF16
             )
             copies.append(z_copy(c, 4 + i, d))
@@ -357,12 +408,12 @@
         for copy in copies[2:]:
             copy.wait()
         for rows, i, j in ((top_half, 3, 4), (low_half, 2, 5)):
-            total = own[rows, lanes]
+            total = own[c][rows, :]
             if nh > 1:
-                total += recv_z[i, :, lanes].astype(F32) + recv_z[j, :, lanes].astype(F32)
-            swap_out[rows, lanes] = total.astype(BF16)
+                total += recv_z[c][i].astype(F32) + recv_z[c][j].astype(F32)
+            swap_out[c][rows, :] = total.astype(BF16)
         copy = remote(
-            swap_out.at[cols(other), lanes], swap_in.at[:, lanes], c_s.at[c], c_r.at[c], at_yc(1)
+            swap_out[c].at[cols(other)], swap_in[c], c_s.at[c], c_r.at[c], at_yc(1)
         )
         copy.start()
         return copy
@@ -370,30 +421,46 @@
     def write(c, copy):
         at, size = chunks[c]
         lanes = slice(at, at + size)
-        mine = swap_out[cols(core), lanes]
-        copy.wait()
-        theirs = swap_in[:, lanes]
+        mine = swap_out[c][cols(core), :]
+        copy.wait()
+        theirs = swap_in[c][...]
         out_ref[:, lanes] = jnp.where(core == 0, mine, theirs)
         dout_ref[:, lanes] = jnp.where(core == 0, theirs, mine)
 
-    last = len(chunks) - 1
-    sends = {}
-    for c in range(last + 1):
-        x_copies = merge(c)
-        if c > 0:
-            forward(c - 1, sends[c - 1])
-        if c == 0:
-            for copy in w_copies:
-                copy.wait()
-            w_local.wait()
-        for copy in x_copies:
-            copy.wait()
-        sends[c] = project(c)
-    swaps = {c: finish(c, sends[c]) for c in range(last)}
-    forward(last, sends[last])
-    for c in range(last):
-        write(c, swaps[c])
-    write(last, finish(last, sends[last]))
+    attend(0, 0, min(1, nz - 1))
+    attend(0, min(1, nz - 1), min(2, nz - 1))
+    attend(0, min(2, nz - 1), min(3, nz - 1))
+    merge_on_way(0)
+    attend(0, min(3, nz - 1), nz)
+    for copy in w_copies:
+        copy.wait()
+    w_copies = [w_relay(d) for d in range(1, ny)]
+    for copy in w_copies:
+        copy.start()
+    attend(1, 0, min(1, nz - 1))
+    attend(1, min(1, nz - 1), min(2, nz - 1))
+    attend(1, min(2, nz - 1), min(3, nz - 1))
+    x_copies_0 = merge(0)
+    attend(1, min(3, nz - 1), nz)
+    merge_on_way(1)
+    for copy in w_copies:
+        copy.wait()
+    w_local.wait()
+    for copy in x_copies_0:
+        copy.wait()
+    sends_0 = project(0)
+    x_copies_1 = merge(1)
+    send(sends_0)
+    forward(0, sends_0)
+    for copy in x_copies_1:
+        copy.wait()
+    sends_1 = project(1)
+    send(sends_1)
+    swap_0 = finish(0, sends_0)
+    forward(1, sends_1)
+    write(0, swap_0)
+    swap_1 = finish(1, sends_1)
+    write(1, swap_1)
 
 
 def hand_over(a_ref, b_ref, out_ref, dout_ref):
@@ -415,6 +482,9 @@
 
     def pair(n):
         return [dma((max(n, 1),)), dma((max(n, 1),))]
+
+    def per_chunk(shape, kind):
+        return [pltpu.VMEM(shape + (size,), kind) for _, size in chunks]
 
     out = jax.ShapeDtypeStruct((col, tok), BF16)
     results = pl.pallas_call(
@@ -431,26 +501,29 @@
             pltpu.VMEM(w.shape, BF16),
             pltpu.VMEM((w.shape[1], HD), BF16),
             pltpu.VMEM((group, peers * HD), BF16),
-            pltpu.VMEM((nz, 2 * HD, tok), BF16),
-            pltpu.VMEM((nz, 8, tok), F32),
-            pltpu.VMEM((max(nz - 1, 1), 2 * HD, tok), BF16),
-            pltpu.VMEM((max(nz - 1, 1), 8, tok), F32),
-            pltpu.VMEM((2, HD, tok), BF16),
-            pltpu.VMEM((peers * HD, tok), BF16),
-            pltpu.VMEM((6, block // 2, tok), BF16),
-            pltpu.VMEM((6, block // 2, tok), BF16),
-            pltpu.VMEM((block // 2, tok), F32),
-            pltpu.VMEM((block // 2, tok), F32),
-            pltpu.VMEM((block, tok), F32),
-            pltpu.VMEM((block, tok), BF16),
-            pltpu.VMEM((col, tok), BF16),
+            per_chunk((nz, 2 * HD), BF16),
+            per_chunk((nz, 8), F32),
+            per_chunk((nz, 2 * HD), BF16),
+            per_chunk((nz, 8), F32),
+            per_chunk((2 * HD,), BF16),
+            per_chunk((8,), F32),
+            per_chunk((2, HD), BF16),
+            per_chunk((peers * HD,), BF16),
+            per_chunk((6, block // 2), BF16),
+            per_chunk((6, block // 2), BF16),
+            per_chunk((block // 2,), F32),
+            per_chunk((block // 2,), F32),
+            per_chunk((block,), F32),
+            per_chunk((block,), BF16),
+            per_chunk((col,), BF16),
         ]
         + pair(4)
         + pair(3)
         + pair(3)
         + pair(2 * ny - 1)
-        + pair(n * (nz - 1))
-        + pair(n * (nz - 1))
+        + pair(n * nz)
+        + pair(n * nz)
+        + [dma((2 * n,))]
         + pair(n * (peers - 1))
         + pair(n * 6)
         + pair(n)

time: 91 us -> 87.3 us (0.959)
  the two profiles are of different devices: /device:TPU:97 before, /device:TPU:9 now
where the time goes in v4:
time: 87.3 us; the launch traced here: 87.1 us
  Pallas kernels  86.5 us (99%)
    pallas_call x1, Pallas kernels, call(): pl.pallas_call(functools.partial(kernel, dims, chunks), out_shape=(out, o...  84.8 us

profile of v4, /device:TPU:9, one launch (start us, length us, event | category | flops | bytes accessed | tf_op | source)
XLA Modules:
  0.0 87.1 jit_solution(18086205821675232124)
XLA Ops:
  0.6 84.8 %attend_and_project.1 = (bf16[160,384]{1,0:T(8,128)(2,1)}, bf16[160,384]{1,0:T(8,128)(2,1)}) custom-call(bf16[384,128]{1,0:T(8,128)(2,1)} %q_ref.1, bf16[384,128]{1,0:T(8,128)(2,1)} %k_ref.1, bf16[384,128]{1,0:T(8,128)(2,1)} %v_ref.1, bf16[384,128]{1,0:T(8,128)(2,1)} %dq_ref.1, bf16[384,128]{1,0:T(8,128)(2,1)} %dk_ref.1, bf16[384,128]{1,0:T(8,128)(2,1)} %dv_ref.1, ...), custom_call_target="tpu_custom_call" | custom-call | tf_op jit(solution)/shard_map/attend_and_project/pallas_call | solution.py:490
  85.5 1.7 %hand_over.1 = (bf16[160,384]{1,0:T(8,128)(2,1)}, bf16[160,384]{1,0:T(8,128)(2,1)}) custom-call(bf16[160,384]{1,0:T(8,128)(2,1)} %get-tuple-element.6.a_ref, bf16[160,384]{1,0:T(8,128)(2,1)} %get-tuple-element.7.b_ref), custom_call_target="tpu_custom_call" | custom-call | tf_op jit(solution)/shard_map/hand_over/pallas_call | solution.py:536

commit v5 on v4

--- a/solution.py
+++ b/solution.py
@@ -430,8 +430,8 @@
     attend(0, 0, min(1, nz - 1))
     attend(0, min(1, nz - 1), min(2, nz - 1))
     attend(0, min(2, nz - 1), min(3, nz - 1))
+    attend(0, min(3, nz - 1), nz)
     merge_on_way(0)
-    attend(0, min(3, nz - 1), nz)
     for copy in w_copies:
         copy.wait()
     w_copies = [w_relay(d) for d in range(1, ny)]

time: 87.3 us -> 86.7 us (level)
  the two profiles are of different devices: /device:TPU:9 before, /device:TPU:1 now
where the time goes in v5:
time: 86.7 us; the launch traced here: 85.1 us
  Pallas kernels  84.5 us (97%)
    pallas_call x1, Pallas kernels, call(): pl.pallas_call(functools.partial(kernel, dims, chunks), out_shape=(out, o...  82.8 us

profile of v5, /device:TPU:1, one launch (start us, length us, event | category | flops | bytes accessed | tf_op | source)
XLA Modules:
  0.0 85.1 jit_solution(10036402936391463484)
XLA Ops:
  0.6 82.8 %attend_and_project.1 = (bf16[160,384]{1,0:T(8,128)(2,1)}, bf16[160,384]{1,0:T(8,128)(2,1)}) custom-call(bf16[384,128]{1,0:T(8,128)(2,1)} %q_ref.1, bf16[384,128]{1,0:T(8,128)(2,1)} %k_ref.1, bf16[384,128]{1,0:T(8,128)(2,1)} %v_ref.1, bf16[384,128]{1,0:T(8,128)(2,1)} %dq_ref.1, bf16[384,128]{1,0:T(8,128)(2,1)} %dk_ref.1, bf16[384,128]{1,0:T(8,128)(2,1)} %dv_ref.1, ...), custom_call_target="tpu_custom_call" | custom-call | tf_op jit(solution)/shard_map/attend_and_project/pallas_call | solution.py:490
  83.4 1.7 %hand_over.1 = (bf16[160,384]{1,0:T(8,128)(2,1)}, bf16[160,384]{1,0:T(8,128)(2,1)}) custom-call(bf16[160,384]{1,0:T(8,128)(2,1)} %get-tuple-element.6.a_ref, bf16[160,384]{1,0:T(8,128)(2,1)} %get-tuple-element.7.b_ref), custom_call_target="tpu_custom_call" | custom-call | tf_op jit(solution)/shard_map/hand_over/pallas_call | solution.py:536
